TPU v7x, 768 devices: a whole 4x8x12 slice. The times are simulated.
768 devices in a mesh: rep: 48 (over z, x_lo, core), blk: 16 (over y, x_hi).
Axes of the slice: x: 4 (x_hi: 2, x_lo: 2; x = x_hi * 2 + x_lo), y: 8, z: 12, core: 2. Of those that a mesh axis runs over, the one named last changes fastest.
Arguments:
- features: bfloat16 [98304, 128], P(('rep', 'blk')), may hold values from -6 to 6
- weight: bfloat16 [128, 128], replicated, may hold values from -0.5 to 0.5
- bias: float32 [128], replicated, may hold values from -3 to 3
- tile_vals: bfloat16 [48, 16, 128, 128, 128], P('rep', 'blk'), may hold values from -0.078125 to 0.078125
- tile_pos: int32 [48, 16, 128], P('rep', 'blk'), may hold values from 0 to 47
- tile_counts: int32 [48, 16, 16], P('rep', 'blk'), may hold values from 1 to 8, as said below
- grad_out: bfloat16 [98304, 128], P(('rep', 'blk')), may hold values from -6 to 6
Outputs:
- activations: bfloat16 [98304, 128], P(('rep', 'blk'))
- grad_weight: float32 [128, 128], replicated
- grad_features: bfloat16 [98304, 128], P(('rep', 'blk'))
Inputs may be any that keep to these rules, and one draw needn't show every extreme that they name: `tile_counts`: on every device some column block has all 8 slots live.
All inputs are finite; a program needn't handle non-finite values.
Results may differ from a plain program's by a relative error of at most 0.02.
Values may be sent and summed in bfloat16 or wider, within the bound.
No kernel may reach another device: no remote copies, remote signals or barrier semaphores. Data moves between devices by JAX's collectives and lax.ppermute only.
A program may use at most 64 MiB of HBM per device.

v0:
```python
import math

import jax
import jax.numpy as jnp
from jax import lax
from jax.sharding import PartitionSpec as P


def shards(features, weight, bias, tile_vals, tile_pos, tile_counts, grad_out):
    replicas = lax.axis_size("rep")
    blocks = lax.axis_size("blk")
    row_count, feature_width = features.shape
    tile_size = tile_vals.shape[-1]
    per_row = row_count // tile_size
    tiles = tile_vals.reshape(tile_vals.shape[2], tile_size, tile_size)
    slot_count = tiles.shape[0] // blocks
    places = tile_pos.reshape(-1)
    counts = tile_counts.reshape(-1)
    slot_ids = jnp.arange(tiles.shape[0], dtype=jnp.int32)
    live_slots = slot_ids % slot_count < counts[slot_ids // slot_count]
    row_tile = places // per_row
    col_tile = places % per_row
    empty = jnp.zeros((replicas * per_row, tile_size, feature_width), jnp.float32)
    shard_rows = lax.all_gather(features, "blk", axis=0, tiled=True)
    block_count = shard_rows.shape[0] // row_count
    shard_tiles = shard_rows.reshape(block_count * per_row, tile_size, feature_width)

    def gather_add_block(block_step, running):
        offset = block_step * slot_count
        values = lax.dynamic_slice_in_dim(tiles, offset, slot_count, 0)
        targets = lax.dynamic_slice_in_dim(row_tile, offset, slot_count, 0)
        sources = block_step * per_row + lax.dynamic_slice_in_dim(col_tile, offset, slot_count, 0)
        live_here = lax.dynamic_slice_in_dim(live_slots, offset, slot_count, 0)
        inputs = jnp.take(shard_tiles, sources, axis=0)
        product = jnp.einsum("sab,sbf->saf", values, inputs, preferred_element_type=jnp.float32)
        product = jnp.where(live_here[:, None, None], product, 0.0)
        return running.at[targets].add(product)

    partial_sum = lax.fori_loop(0, block_count, gather_add_block, empty)
    aggregate = lax.psum_scatter(
        partial_sum.reshape(replicas * row_count, feature_width),
        "rep",
        scatter_dimension=0,
        tiled=True,
    )
    aggregate_bf = aggregate.astype(jnp.bfloat16)
    pre = jnp.dot(aggregate_bf, weight, preferred_element_type=jnp.float32) + bias
    activations = jax.nn.elu(pre).astype(jnp.bfloat16)
    slope = jnp.where(pre > 0, 1.0, jnp.exp(jnp.minimum(pre, 0.0)))
    grad_pre = (grad_out.astype(jnp.float32) * slope).astype(jnp.bfloat16)
    local_weight = lax.dot_general(
        aggregate_bf, grad_pre, (((0,), (0,)), ((), ())), preferred_element_type=jnp.float32
    )
    node_total = row_count * replicas * blocks
    grad_weight = lax.psum(local_weight, ("rep", "blk")) / math.sqrt(node_total)
    product = lax.dot_general(
        grad_pre, weight, (((1,), (1,)), ((), ())), preferred_element_type=jnp.float32
    )
    gathered = lax.all_gather(product.astype(jnp.bfloat16), "rep", axis=0, tiled=True)
    gathered_tiles = gathered.reshape(replicas * per_row, tile_size, feature_width)
    span = row_count * lax.axis_size("blk")
    block_count = span // row_count

    def column_add_block(block_step, columns):
        offset = block_step * slot_count
        values = lax.dynamic_slice_in_dim(tiles, offset, slot_count, 0)
        targets = lax.dynamic_slice_in_dim(row_tile, offset, slot_count, 0)
        sources = lax.dynamic_slice_in_dim(col_tile, offset, slot_count, 0)
        blank = jnp.zeros((per_row, tile_size, feature_width), jnp.float32)
        live_here = lax.dynamic_slice_in_dim(live_slots, offset, slot_count, 0)
        inputs = jnp.take(gathered_tiles, targets, axis=0)
        product = jnp.einsum("sab,saf->sbf", values, inputs, preferred_element_type=jnp.float32)
        product = jnp.where(live_here[:, None, None], product, 0.0)
        column_block = blank.at[sources].add(product)
        return lax.dynamic_update_slice_in_dim(columns, column_block, block_step * per_row, 0)

    start_columns = jnp.zeros((block_count * per_row, tile_size, feature_width), jnp.float32)
    columns = lax.fori_loop(0, block_count, column_add_block, start_columns)
    grad_features = lax.psum_scatter(
        columns.reshape(span, feature_width).astype(jnp.bfloat16),
        "blk",
        scatter_dimension=0,
        tiled=True,
    )
    return (activations, grad_weight, grad_features)


def solution(mesh):
    in_specs = (
        P(("rep", "blk"), None),
        P(),
        P(),
        P("rep", "blk", None, None, None),
        P("rep", "blk", None),
        P("rep", "blk", None),
        P(("rep", "blk"), None),
    )
    out_specs = (P(("rep", "blk"), None), P(), P(("rep", "blk"), None))
    return jax.shard_map(shards, mesh=mesh, in_specs=in_specs, out_specs=out_specs, check_vma=False)
```

profile of v0, /device:TPU:16, one launch (start us, length us, event | category | flops | bytes accessed | tf_op | source)
XLA Modules:
  0.0 1090.2 jit_solution(6658917042709469817)
XLA Ops:
  7.2 2.0 fusion.23
  9.2 43.7 %all_gather.6 = bf16[2048,128]{1,0:T(8,128)(2,1)S(1)} all-gather(bf16[128,128]{1,0:T(8,128)(2,1)} %param.11), channel_id=1, replica_groups=mesh['rep'=48,'blk'=16] {'blk'}, dimensions={0}, use_global_device_ids=true | all-gather | bytes 557056 | tf_op jit(solution)/shard_map/all_gather | solution.py:24
  52.9 10.0 fusion.19
  62.9 2.0 broadcast_in_dim.146
  64.9 74.2 %while.28 = (s32[]{:T(128)}, f32[48,128,128]{2,1,0:T(8,128)}, s32[128]{0:T(128)S(1)}, pred[128]{0:T(512)(128)(4,1)S(1)}, bf16[128,128,128]{2,1,0:T(8,128)(2,1)},...) while((s32[]{:T(128)}, f32[48,128,128]{2,1,0:T(8,128)}, ...), condition=%wide.region_2.3_spmd, body=%wide.region_0.2_spmd.sunk | while | flops 33948704 | bytes 3150233 | solution.py:39
  66.8 2.7 scatter_fusion
  71.5 2.7 scatter_fusion
  76.1 2.7 scatter_fusion
  80.8 2.7 scatter_fusion
  85.4 2.7 scatter_fusion
  90.1 2.7 scatter_fusion
  94.7 2.6 scatter_fusion
  99.3 2.7 scatter_fusion
  103.9 2.7 scatter_fusion
  108.6 2.7 scatter_fusion
  113.3 2.7 scatter_fusion
  117.9 2.7 scatter_fusion
  122.5 2.7 scatter_fusion
  127.2 2.7 scatter_fusion
  131.8 2.7 scatter_fusion
  136.5 2.7 scatter_fusion
  139.2 182.2 %reduce-scatter.3.cloned.1.call-done = f32[128,128]{1,0:T(8,128)} async-done(((f32[6144,128]{1,0:T(8,128)}), f32[128,128]{1,0:T(8,128)}) %reduce-scatter.3.cloned.1.call-update) | async-done | bytes 65552 | tf_op jit(solution)/shard_map/reduce_scatter | solution.py:40
  321.4 1.6 fusion.13
  323.9 6.4 copy.10
  331.1 87.3 %all-gather.2.cloned.1.call-done = bf16[6144,128]{1,0:T(8,128)(2,1)} async-done(((bf16[128,128]{1,0:T(8,128)(2,1)}), bf16[6144,128]{1,0:T(8,128)(2,1)}) %all-gather.2.cloned.1.call-update) | async-done | bytes 1572880 | tf_op jit(solution)/shard_map/all_gather | solution.py:59
  418.4 81.0 %while.29 = (s32[]{:T(128)}, bf16[16,128,128]{2,1,0:T(8,128)(2,1)}, pred[128]{0:T(512)(128)(4,1)S(1)}, bf16[128,128,128]{1,2,0:T(8,128)(2,1)}, s32[128]{0:T(128)...) while((s32[]{:T(128)}, bf16[16,128,128]{2,1,0:T(8,128)(2,1)}, ...), condition=%wide.region_7.8_spmd, body=%wide.region_5.7_spmd.sunk | while | flops 33948724 | bytes 3347351 | solution.py:78
  418.5 2.0 gather_fusion.1
  423.6 2.0 gather_fusion.1
  425.7 1.2 convolution_select_fusion.5
  428.6 2.0 gather_fusion.1
  433.7 2.0 gather_fusion.1
  435.8 1.2 convolution_select_fusion.5
  438.8 2.0 gather_fusion.1
  443.8 2.0 gather_fusion.1
  448.9 2.0 gather_fusion.1
  451.0 1.2 convolution_select_fusion.5
  454.0 2.0 gather_fusion.1
  459.0 2.0 gather_fusion.1
  464.1 2.0 gather_fusion.1
  469.1 2.0 gather_fusion.1
  474.2 2.0 gather_fusion.1
  479.3 2.0 gather_fusion.1
  484.3 2.0 gather_fusion.1
  489.4 2.0 gather_fusion.1
  494.4 2.0 gather_fusion.1
  499.4 375.2 %all-reduce.2.cloned.1.call-done = f32[128,128]{1,0:T(8,128)} async-done(((f32[128,128]{1,0:T(8,128)}), f32[128,128]{1,0:T(8,128)}) %all-reduce.2.cloned.1.call-update) | async-done | bytes 65552 | tf_op jit(solution)/shard_map/psum | solution.py:55
  874.6 1.5 broadcast_multiply_fusion
  876.1 207.6 %reduce-scatter.5.cloned.1.call-done = bf16[128,128]{1,0:T(8,128)(2,1)} async-done(((bf16[2048,128]{1,0:T(8,128)(2,1)}), bf16[128,128]{1,0:T(8,128)(2,1)}) %reduce-scatter.5.cloned.1.call-update) | async-done | bytes 32784 | tf_op jit(solution)/shard_map/reduce_scatter | solution.py:79
  (242 shorter events, 77.3 us)
Async XLA Ops:
  7.2 314.2 %copy-start = (bf16[128,128]{1,0:T(8,128)(2,1)S(1)}, bf16[128,128]{1,0:T(8,128)(2,1)}, u32[]{:S(2)}) copy-start(bf16[128,128]{1,0:T(8,128)(2,1)} %param.12) | copy-start | bytes 98308
  7.2 57.7 %copy-start.3 = (s32[1,1,128]{2,1,0:T(1,128)S(1)}, s32[1,1,128]{2,1,0:T(1,128)}, u32[]{:S(2)}) copy-start(s32[1,1,128]{2,1,0:T(1,128)} %param.15) | copy-start | bytes 1540
  7.2 314.2 %reduce-scatter.3.cloned.1.call-start = ((), (), s32[]{:S(2)}) async-start(), calls=%async_computation.2 | async-start | bytes 3211264 | tf_op jit(solution)/shard_map/reduce_scatter | solution.py:40
  139.1 182.2 %copy-start.4 = (f32[128]{0:T(128)S(1)}, f32[128]{0:T(128)}, u32[]{:S(2)}) copy-start(f32[128]{0:T(128)} %param.13) | copy-start | bytes 1540
  139.1 183.9 %copy-start.2 = (bf16[128,128]{1,0:T(8,128)(2,1)S(1)}, bf16[128,128]{1,0:T(8,128)(2,1)}, u32[]{:S(2)}) copy-start(bf16[128,128]{1,0:T(8,128)(2,1)} %param.17) | copy-start | bytes 98308
  139.2 279.3 %all-gather.2.cloned.1.call-start = ((), (), s32[]{:S(2)}) async-start(), calls=%async_computation.4 | async-start | bytes 1605632 | tf_op jit(solution)/shard_map/all_gather | solution.py:59
  323.8 6.4 copy-start.1
  323.8 550.8 %all-reduce.2.cloned.1.call-start = ((), (), s32[]{:S(2)}) async-start(), calls=%async_computation.3 | async-start | bytes 131072 | tf_op jit(solution)/shard_map/psum | solution.py:55
  331.1 752.7 %reduce-scatter.5.cloned.1.call-start = ((), (), s32[]{:S(2)}) async-start(), calls=%async_computation.5 | async-start | bytes 557056 | tf_op jit(solution)/shard_map/reduce_scatter | solution.py:79
Sparse Core Ops, SparseCore 0:
  139.3 182.0 reduce-scatter.2
  324.8 93.6 all-gather.1
  425.3 449.2 all-reduce.1
  880.0 203.6 reduce-scatter.4
where the time goes:
time: 1090 us
  waiting for transfers between devices  852 us (78%)
  other arithmetic  73 us (7%)
  local copies, waits for them, and re-layouts  64.5 us (6%)
  blocking collectives  43.7 us (4%)
  matrix products  41.9 us (4%)
  between operations  13.8 us (1%)
    psum x1, waiting for transfers between devices, shards(): grad_weight = lax.psum(local_weight, ('rep', 'blk')) / math.sqrt(node_total)  375 us
    reduce_scatter x1, waiting for transfers between devices, shards(): lax.psum_scatter(columns.reshape(span, feature_width).astype(jnp.bfloat16...  208 us
    reduce_scatter x1, waiting for transfers between devices, shards(): lax.psum_scatter(partial_sum.reshape(replicas * row_count, feature_width)...  182 us
    all_gather x1, waiting for transfers between devices, shards(): lax.all_gather(product.astype(jnp.bfloat16), 'rep', axis=0, tiled=True)  87.3 us
    all_gather x1, blocking collectives, shards(): shard_rows = lax.all_gather(features, 'blk', axis=0, tiled=True)  43.7 us
    scatter-add x16, other arithmetic, gather_add_block(): return running.at[targets].add(product)  43 us
    gather x16, local copies, waits for them, and re-layouts, column_add_block(): inputs = jnp.take(gathered_tiles, targets, axis=0)  32.1 us
  transfers between devices with their start and end apart: 4, of which 4 were waited for; matrix products, arithmetic and copies ran while one was open for 8% of the time, Pallas kernels for 0%

commit v1 on v0

v1 whole, which is shorter than its diff:
```python
import functools
import math

import jax
import jax.numpy as jnp
from jax import lax
from jax.experimental import pallas as pl
from jax.experimental.pallas import tpu as pltpu
from jax.sharding import Mesh, PartitionSpec as P

AXES = ("z", "x_lo", "core", "y", "x_hi")
REP = ("z", "x_lo", "core")
BLK = ("y", "x_hi")
BF16 = jnp.bfloat16
F32 = jnp.float32
VMEM = pl.BlockSpec(memory_space=pltpu.VMEM)
SMEM = pl.BlockSpec(memory_space=pltpu.SMEM)
LIMIT = 24 * 1024 * 1024


def place_of(pos, mine, z_count):
    differs = pos ^ mine
    return ((differs & 1) * 2 + ((differs >> 1) & 1)) * z_count + (pos >> 2)


def forward_kernel(z_count, slots, mine_ref, pos_ref, counts_ref, tiles_ref, rows_ref, send_ref, keep_ref, acc_ref):
    blocks, tile, width = rows_ref.shape
    half = 2 * z_count
    acc_ref[...] = jnp.zeros_like(acc_ref)
    mine = mine_ref[0]

    def block_step(j, carry):
        base = j * slots
        values = tiles_ref[pl.ds(base, slots)].reshape(slots * tile, tile)
        product = jnp.dot(values, rows_ref[j], preferred_element_type=F32)
        count = counts_ref[0, 0, j]
        for s in range(slots):
            place = place_of(pos_ref[0, 0, base + s], mine, z_count)
            place = jnp.where(s < count, place, 2 * half)
            acc_ref[place] += product[s * tile : (s + 1) * tile]
        return carry

    lax.fori_loop(0, blocks, block_step, 0)
    keep_ref[...] = acc_ref[0:half]
    send_ref[...] = acc_ref[half : 2 * half].astype(BF16)


def dense_kernel(parts_ref, weight_ref, bias_ref, grad_ref, act_ref, out_ref):
    tile = grad_ref.shape[0]
    total = parts_ref[0].astype(F32)
    for z in range(1, parts_ref.shape[0]):
        total += parts_ref[z].astype(F32)
    aggregate = total.astype(BF16)
    pre = jnp.dot(aggregate, weight_ref[...], preferred_element_type=F32) + bias_ref[...]
    low = jnp.exp(jnp.minimum(pre, 0.0))
    act_ref[...] = jnp.where(pre > 0, pre, low - 1.0).astype(BF16)
    slope = jnp.where(pre > 0, 1.0, low)
    grad_pre = (grad_ref[...].astype(F32) * slope).astype(BF16)
    out_ref[0:tile] = lax.dot_general(
        weight_ref[...], grad_pre, (((1,), (1,)), ((), ())), preferred_element_type=F32
    ).astype(BF16)
    out_ref[tile:] = lax.dot_general(
        aggregate, grad_pre, (((0,), (0,)), ((), ())), preferred_element_type=F32
    ).astype(BF16)


def backward_kernel(
    z_count, slots, mine_ref, pos_ref, counts_ref, tiles_ref, a_ref, b_ref, c_ref, d_ref, out_ref, held_ref
):
    blocks = out_ref.shape[0]
    tile = tiles_ref.shape[1]
    weight = jnp.zeros((tile, tile), F32)
    for n, ref in enumerate((a_ref, b_ref, c_ref, d_ref)):
        held_ref[n * z_count : (n + 1) * z_count] = ref[0:z_count]
        weight += ref[z_count].astype(F32)
    weight = weight.astype(BF16)
    held_ref[4 * z_count] = jnp.zeros((tile, tile), BF16)
    mine = mine_ref[0]

    def block_step(j, carry):
        base = j * slots
        count = counts_ref[0, 0, j]
        picked = []
        for s in range(slots):
            place = place_of(pos_ref[0, 0, base + s], mine, z_count)
            place = jnp.where(s < count, place, 4 * z_count)
            picked.append(held_ref[place])
        left = jnp.concatenate(picked, axis=1)
        values = tiles_ref[pl.ds(base, slots)].reshape(slots * tile, tile)
        out_ref[j, 0:tile] = jnp.dot(left, values, preferred_element_type=F32).astype(BF16)
        out_ref[j, tile:] = weight
        return carry

    lax.fori_loop(0, blocks, block_step, 0)


def finish_kernel(scale, parts_ref, grad_ref, weight_ref):
    tile = grad_ref.shape[0]
    total = parts_ref[0].astype(F32)
    for n in range(1, parts_ref.shape[0]):
        total += parts_ref[n].astype(F32)
    grad_ref[...] = total[0:tile].T.astype(BF16)
    weight_ref[...] = total[tile:] * scale


def shards(features, weight, bias, tile_vals, tile_pos, tile_counts, grad_out):
    z_count = lax.axis_size("z")
    blocks = lax.axis_size(BLK)
    tile, width = features.shape
    tiles = tile_vals.reshape(tile_vals.shape[2:])
    slots = tiles.shape[0] // blocks
    nodes = tile * lax.axis_size(AXES)
    mine = (lax.axis_index("x_lo") * 2 + lax.axis_index("core")).astype(jnp.int32).reshape(1)
    params = pltpu.CompilerParams(vmem_limit_bytes=LIMIT)
    swap = [(0, 1), (1, 0)]

    rows = lax.all_to_all(jnp.broadcast_to(features[None], (blocks, tile, width)), BLK, 0, 0, tiled=True)
    send, keep = pl.pallas_call(
        functools.partial(forward_kernel, z_count, slots),
        out_shape=(
            jax.ShapeDtypeStruct((2 * z_count, tile, width), BF16),
            jax.ShapeDtypeStruct((2 * z_count, tile, width), F32),
        ),
        in_specs=[SMEM, SMEM, SMEM, VMEM, VMEM],
        out_specs=(VMEM, VMEM),
        scratch_shapes=[pltpu.VMEM((4 * z_count + 1, tile, width), F32)],
        compiler_params=params,
        name="forward",
    )(mine, tile_pos, tile_counts, tiles, rows)
    got = lax.ppermute(send, "core", swap)
    send = (keep[z_count:] + got[z_count:].astype(F32)).astype(BF16)
    keep = keep[:z_count] + got[:z_count].astype(F32)
    got = lax.ppermute(send, "x_lo", swap)
    parts = lax.all_to_all((keep + got.astype(F32)).astype(BF16), "z", 0, 0, tiled=True)

    activations, packed = pl.pallas_call(
        dense_kernel,
        out_shape=(
            jax.ShapeDtypeStruct((tile, width), BF16),
            jax.ShapeDtypeStruct((2 * tile, width), BF16),
        ),
        in_specs=[VMEM] * 4,
        out_specs=(VMEM, VMEM),
        compiler_params=params,
        name="dense",
    )(parts, weight, bias.reshape(1, -1), grad_out)

    gathered = lax.all_gather(packed, "z", axis=0)
    held = jnp.concatenate(
        [gathered[:, :tile], gathered[:, tile:].astype(F32).sum(0, keepdims=True).astype(BF16)], axis=0
    )
    held_x = lax.ppermute(held, "x_lo", swap)
    held_c = lax.ppermute(held, "core", swap)
    held_xc = lax.ppermute(held_x, "core", swap)
    chunks = pl.pallas_call(
        functools.partial(backward_kernel, z_count, slots),
        out_shape=jax.ShapeDtypeStruct((blocks, 2 * tile, width), BF16),
        in_specs=[SMEM, SMEM, SMEM] + [VMEM] * 5,
        out_specs=VMEM,
        scratch_shapes=[pltpu.VMEM((4 * z_count + 1, tile, width), BF16)],
        compiler_params=params,
        name="backward",
    )(mine, tile_pos, tile_counts, tiles, held, held_x, held_c, held_xc)
    parts = lax.all_to_all(chunks, BLK, 0, 0, tiled=True)
    grad_features, grad_weight = pl.pallas_call(
        functools.partial(finish_kernel, 1.0 / math.sqrt(nodes)),
        out_shape=(
            jax.ShapeDtypeStruct((tile, width), BF16),
            jax.ShapeDtypeStruct((width, width), F32),
        ),
        in_specs=[VMEM],
        out_specs=(VMEM, VMEM),
        compiler_params=params,
        name="finish",
    )(parts)
    return (activations, grad_weight, grad_features)


def solution(mesh):
    reps, blks = mesh.devices.shape
    fine = Mesh(mesh.devices.reshape(reps // 4, 2, 2, blks // 2, 2), AXES)
    in_specs = (
        P(AXES, None),
        P(),
        P(),
        P(REP, BLK, None, None, None),
        P(REP, BLK, None),
        P(REP, BLK, None),
        P(AXES, None),
    )
    out_specs = (P(AXES, None), P(), P(AXES, None))
    return jax.shard_map(shards, mesh=fine, in_specs=in_specs, out_specs=out_specs, check_vma=False)
```

time: 1090 us -> 169 us (0.16)
  the two profiles are of different devices: /device:TPU:16 before, /device:TPU:2 now
where the time goes in v1:
time: 169 us; the launch traced here: 168 us
  blocking collectives  94.4 us (56%)
  waiting for transfers between devices  37 us (22%)
  starting transfers between devices  21.4 us (13%)
  Pallas kernels  10.6 us (6%)
  local copies, waits for them, and re-layouts  3.88 us (2%)
    all_to_all x1, blocking collectives, shards(): lax.all_to_all((keep + got.astype(F32)).astype(BF16), 'z', 0, 0, tiled=True)  34.5 us
    all_to_all x1, blocking collectives, shards(): parts = lax.all_to_all(chunks, BLK, 0, 0, tiled=True)  33.6 us
    all_gather x1, blocking collectives, shards(): gathered = lax.all_gather(packed, 'z', axis=0)  26.4 us
    all_to_all x1, waiting for transfers between devices, shards(): lax.all_to_all(jnp.broadcast_to(features[None], (blocks, tile, width)), B...  18.7 us
    ppermute x1, waiting for transfers between devices, shards(): got = lax.ppermute(send, 'x_lo', swap)  9.65 us
    all_to_all x1, starting transfers between devices, shards(): lax.all_to_all(jnp.broadcast_to(features[None], (blocks, tile, width)), B...  8.77 us
    pallas_call x1, Pallas kernels, shards(): pl.pallas_call(functools.partial(forward_kernel, z_count, slots), out_sha...  4.83 us
    ppermute x1, waiting for transfers between devices, shards(): held_x = lax.ppermute(held, 'x_lo', swap)  4.71 us
  transfers between devices with their start and end apart: 6, of which 5 were waited for; matrix products, arithmetic and copies ran while one was open for 0% of the time, Pallas kernels for 0%

profile of v1, /device:TPU:2, one launch (start us, length us, event | category | flops | bytes accessed | tf_op | source)
XLA Modules:
  0.0 168.5 jit_solution(234813006084115480)
XLA Ops:
  0.6 0.0 copy-start.5
  0.6 0.0 copy-start.4
  0.7 1.7 broadcast_in_dim.2
  2.3 8.8 %all-to-all-start = ((bf16[16,128,128]{2,1,0:T(8,128)(2,1)}), bf16[16,128,128]{2,1,0:T(8,128)(2,1)S(1)}, u32[]{:S(2)}, u32[]{:S(2)}) async-start(bf16[16,128,128]{2,1,0:T(8,128)(2,1)} %broadcast_in_dim.2), calls=%async_computation | async-start | bytes 1048576 | tf_op jit(solution)/shard_map/all_to_all | solution.py:117
  11.1 18.7 %all-to-all-done.rows_ref = bf16[16,128,128]{2,1,0:T(8,128)(2,1)S(1)} async-done(((bf16[16,128,128]{2,1,0:T(8,128)(2,1)}), bf16[16,128,128]{2,1,0:T(8,128)(2,1)S(1)}, u32[]{:S(2)}, u32[]{:S(2)}) %all-to-all-start) | async-done | bytes 524320 | tf_op jit(solution)/shard_map/all_to_all | solution.py:117
  29.7 0.0 copy-done.5
  29.7 0.0 copy-done.4
  29.8 0.0 copy-start
  29.8 2.2 %copy-done = bf16[1,1,128,128,128]{4,3,2,1,0:T(8,128)(2,1)S(1)} copy-done((bf16[1,1,128,128,128]{4,3,2,1,0:T(8,128)(2,1)S(1)}, bf16[1,1,128,128,128]{4,3,2,1,0:T(8,128)(2,1)}, u32[]{:S(2)}) %copy-start) | copy-done | bytes 4194328
  31.9 4.8 %forward.1 = (bf16[24,128,128]{2,1,0:T(8,128)(2,1)S(1)}, f32[24,128,128]{2,1,0:T(8,128)S(1)}) custom-call(s32[1]{0:T(128)} %bitcast.mine_ref, s32[1,1,128]{2,1,0:T(1,128)S(1)} %copy-done.4, s32[1,1,16]{2,1,0:T(1,128)S(1)} %copy-done.5, bf16[128,128,128]{2,1,0:T(8,128)(2,1)S(1)} %bitcast.5, bf16[16,128,128]{2,1,0:T(8,128)(2,1)S(1)} %all-to-all-done.rows_ref), custom_call_target="tpu_custom_call" | custom-call | tf_op jit(solution)/shard_map/forward/pallas_call | solution.py:118
  36.8 1.9 %collective-permute-start = (bf16[24,128,128]{2,1,0:T(8,128)(2,1)S(1)}, bf16[24,128,128]{2,1,0:T(8,128)(2,1)S(1)}, u32[]{:S(2)}, u32[]{:S(2)}) collective-permute-start(bf16[24,128,128]{2,1,0:T(8,128)(2,1)S(1)} %get-tuple-element.10), channel_id=1, source_target_pairs={{0,16},{16,0},{1,17},{17,1},{2,18},{18,2},{3,19},{19,3},{4,20},{20... | collective-permute-start | bytes 2359304 | tf_op jit(solution)/shard_map/ppermute | solution.py:130
  38.7 2.3 %collective-permute-done = bf16[24,128,128]{2,1,0:T(8,128)(2,1)S(1)} collective-permute-done((bf16[24,128,128]{2,1,0:T(8,128)(2,1)S(1)}, bf16[24,128,128]{2,1,0:T(8,128)(2,1)S(1)}, u32[]{:S(2)}, u32[]{:S(2)}) %collective-permute-start) | collective-permute-done | bytes 786464 | tf_op jit(solution)/shard_map/ppermute | solution.py:130
  41.0 0.1 add_convert_fusion.1
  41.1 0.0 copy-start.2
  41.1 0.0 copy-start.3
  41.1 0.0 copy-start.6
  41.1 3.5 %collective-permute-start.1 = (bf16[12,128,128]{2,1,0:T(8,128)(2,1)S(1)}, bf16[12,128,128]{2,1,0:T(8,128)(2,1)S(1)}, u32[]{:S(2)}, u32[]{:S(2)}) collective-permute-start(bf16[12,128,128]{2,1,0:T(8,128)(2,1)S(1)} %add_convert_fusion.1), channel_id=1, source_target_pairs={{0,32},{32,0},{1,33},{33,1},{2,34},{34,2},{3,35},{35,3},{4,36},{36... | collective-permute-start | bytes 1179656 | tf_op jit(solution)/shard_map/ppermute | solution.py:133
  44.6 9.6 %collective-permute-done.1 = bf16[12,128,128]{2,1,0:T(8,128)(2,1)S(1)} collective-permute-done((bf16[12,128,128]{2,1,0:T(8,128)(2,1)S(1)}, bf16[12,128,128]{2,1,0:T(8,128)(2,1)S(1)}, u32[]{:S(2)}, u32[]{:S(2)}) %collective-permute-start.1) | collective-permute-done | bytes 393248 | tf_op jit(solution)/shard_map/ppermute | solution.py:133
  54.3 0.0 copy-start.1
  54.3 0.1 add_convert_fusion
  54.4 34.5 %all_to_all.15.parts_ref = bf16[12,128,128]{2,1,0:T(8,128)(2,1)S(1)} all-to-all(bf16[12,128,128]{2,1,0:T(8,128)(2,1)S(1)} %add_convert_fusion), channel_id=1, replica_groups=mesh['z'=12,'x_lo'=2,'core'=2,'y'=8,'x_hi'=2] {'z'}, dimensions={0} | all-to-all | bytes 786432 | tf_op jit(solution)/shard_map/all_to_all | solution.py:134
  88.9 0.0 copy-done.2
  88.9 0.0 copy-done.3
  88.9 0.0 copy-done.6
  88.9 0.8 dense.1
  89.7 26.4 %all-gather = bf16[3072,128]{1,0:T(8,128)(2,1)S(1)} all-gather(bf16[256,128]{1,0:T(8,128)(2,1)S(1)} %get-tuple-element.12), channel_id=2, replica_groups=mesh['z'=12,'x_lo'=2,'core'=2,'y'=8,'x_hi'=2] {'z'}, dimensions={0}, use_global_device_ids=true | all-gather | bytes 851968 | tf_op jit(solution)/shard_map/all_gather | solution.py:148
  116.1 0.1 fusion
  116.2 3.4 %collective-permute-start.2 = (bf16[13,128,128]{2,1,0:T(8,128)(2,1)S(1)}, bf16[13,128,128]{2,1,0:T(8,128)(2,1)S(1)}, u32[]{:S(2)}, u32[]{:S(2)}) collective-permute-start(bf16[13,128,128]{2,1,0:T(8,128)(2,1)S(1)} %pad_maximum_fusion.a_ref), channel_id=1, source_target_pairs={{0,32},{32,0},{1,33},{33,1},{2,34},{34,2},{3,35},{35,3},{4,36},{36... | collective-permute-start | bytes 1277960 | tf_op jit(solution)/shard_map/ppermute | solution.py:152
  119.6 1.9 %collective-permute-start.3 = (bf16[13,128,128]{2,1,0:T(8,128)(2,1)S(1)}, bf16[13,128,128]{2,1,0:T(8,128)(2,1)S(1)}, u32[]{:S(2)}, u32[]{:S(2)}) collective-permute-start(bf16[13,128,128]{2,1,0:T(8,128)(2,1)S(1)} %pad_maximum_fusion.a_ref), channel_id=1, source_target_pairs={{0,16},{16,0},{1,17},{17,1},{2,18},{18,2},{3,19},{19,3},{4,20},{20... | collective-permute-start | bytes 1277960 | tf_op jit(solution)/shard_map/ppermute | solution.py:153
  121.5 4.7 %collective-permute-done.2.b_ref = bf16[13,128,128]{2,1,0:T(8,128)(2,1)S(1)} collective-permute-done((bf16[13,128,128]{2,1,0:T(8,128)(2,1)S(1)}, bf16[13,128,128]{2,1,0:T(8,128)(2,1)S(1)}, u32[]{:S(2)}, u32[]{:S(2)}) %collective-permute-start.2) | collective-permute-done | bytes 426016 | tf_op jit(solution)/shard_map/ppermute | solution.py:152
  126.2 1.9 %collective-permute-start.4 = (bf16[13,128,128]{2,1,0:T(8,128)(2,1)S(1)}, bf16[13,128,128]{2,1,0:T(8,128)(2,1)S(1)}, u32[]{:S(2)}, u32[]{:S(2)}) collective-permute-start(bf16[13,128,128]{2,1,0:T(8,128)(2,1)S(1)} %collective-permute-done.2.b_ref), channel_id=1, source_target_pairs={{0,16},{16,0},{1,17},{17,1},{2,18},{18,2},{3,19},{19,3},{4,20},{20... | collective-permute-start | bytes 1277960 | tf_op jit(solution)/shard_map/ppermute | solution.py:154
  128.1 0.0 collective-permute-done.3.c_ref
  128.2 1.7 %collective-permute-done.4.d_ref = bf16[13,128,128]{2,1,0:T(8,128)(2,1)S(1)} collective-permute-done((bf16[13,128,128]{2,1,0:T(8,128)(2,1)S(1)}, bf16[13,128,128]{2,1,0:T(8,128)(2,1)S(1)}, u32[]{:S(2)}, u32[]{:S(2)}) %collective-permute-start.4) | collective-permute-done | bytes 426016 | tf_op jit(solution)/shard_map/ppermute | solution.py:154
  129.9 0.0 copy-done.1
  129.9 4.2 %backward.1 = bf16[16,256,128]{2,1,0:T(8,128)(2,1)S(1)} custom-call(s32[1]{0:T(128)} %bitcast.mine_ref, s32[1,1,128]{2,1,0:T(1,128)S(1)} %copy-done.4, s32[1,1,16]{2,1,0:T(1,128)S(1)} %copy-done.5, bf16[128,128,128]{2,1,0:T(8,128)(2,1)S(1)} %bitcast.6, bf16[13,128,128]{2,1,0:T(8,128)(2,1)S(1)} %pad_maximum_fusion.a_ref, ...), custom_call_target="tpu_custom_call" | custom-call | tf_op jit(solution)/shard_map/backward/pallas_call | solution.py:155
  134.1 33.6 %all_to_all.16.parts_ref = bf16[16,256,128]{2,1,0:T(8,128)(2,1)S(1)} all-to-all(bf16[16,256,128]{2,1,0:T(8,128)(2,1)S(1)} %backward.1), channel_id=1, replica_groups=mesh['z'=12,'x_lo'=2,'core'=2,'y'=8,'x_hi'=2] {'y','x_hi'}, dimensions={0} | all-to-all | bytes 2097152 | tf_op jit(solution)/shard_map/all_to_all | solution.py:164
  167.7 0.8 finish.1
  (1 shorter events, 0.0 us)
Async XLA Ops:
  0.6 29.1 %copy-start.5 = (s32[1,1,16]{2,1,0:T(1,128)S(1)}, s32[1,1,16]{2,1,0:T(1,128)}, u32[]{:S(2)}) copy-start(s32[1,1,16]{2,1,0:T(1,128)} %counts_ref.3) | copy-start | bytes 196
  0.6 29.1 %copy-start.4 = (s32[1,1,128]{2,1,0:T(1,128)S(1)}, s32[1,1,128]{2,1,0:T(1,128)}, u32[]{:S(2)}) copy-start(s32[1,1,128]{2,1,0:T(1,128)} %pos_ref.3) | copy-start | bytes 1540
  2.3 27.4 %all-to-all-start = ((bf16[16,128,128]{2,1,0:T(8,128)(2,1)}), bf16[16,128,128]{2,1,0:T(8,128)(2,1)S(1)}, u32[]{:S(2)}, u32[]{:S(2)}) async-start(bf16[16,128,128]{2,1,0:T(8,128)(2,1)} %broadcast_in_dim.2), calls=%async_computation | async-start | bytes 1048576 | tf_op jit(solution)/shard_map/all_to_all | solution.py:117
  29.8 2.2 %copy-start = (bf16[1,1,128,128,128]{4,3,2,1,0:T(8,128)(2,1)S(1)}, bf16[1,1,128,128,128]{4,3,2,1,0:T(8,128)(2,1)}, u32[]{:S(2)}) copy-start(bf16[1,1,128,128,128]{4,3,2,1,0:T(8,128)(2,1)} %param.10) | copy-start | bytes 12582916
  36.8 4.2 %collective-permute-start = (bf16[24,128,128]{2,1,0:T(8,128)(2,1)S(1)}, bf16[24,128,128]{2,1,0:T(8,128)(2,1)S(1)}, u32[]{:S(2)}, u32[]{:S(2)}) collective-permute-start(bf16[24,128,128]{2,1,0:T(8,128)(2,1)S(1)} %get-tuple-element.10), channel_id=1, source_target_pairs={{0,16},{16,0},{1,17},{17,1},{2,18},{18,2},{3,19},{19,3},{4,20},{20... | collective-permute-start | bytes 2359304 | tf_op jit(solution)/shard_map/ppermute | solution.py:130
  41.1 47.9 %copy-start.2 = (bf16[128,128]{1,0:T(8,128)(2,1)S(1)}, bf16[128,128]{1,0:T(8,128)(2,1)}, u32[]{:S(2)}) copy-start(bf16[128,128]{1,0:T(8,128)(2,1)} %weight_ref.1) | copy-start | bytes 98308
  41.1 47.8 %copy-start.3 = (bf16[128,128]{1,0:T(8,128)(2,1)S(1)}, bf16[128,128]{1,0:T(8,128)(2,1)}, u32[]{:S(2)}) copy-start(bf16[128,128]{1,0:T(8,128)(2,1)} %grad_ref.1) | copy-start | bytes 98308
  41.1 47.8 %copy-start.6 = (f32[128]{0:T(128)S(1)}, f32[128]{0:T(128)}, u32[]{:S(2)}) copy-start(f32[128]{0:T(128)} %param.9) | copy-start | bytes 1540
  41.1 13.2 %collective-permute-start.1 = (bf16[12,128,128]{2,1,0:T(8,128)(2,1)S(1)}, bf16[12,128,128]{2,1,0:T(8,128)(2,1)S(1)}, u32[]{:S(2)}, u32[]{:S(2)}) collective-permute-start(bf16[12,128,128]{2,1,0:T(8,128)(2,1)S(1)} %add_convert_fusion.1), channel_id=1, source_target_pairs={{0,32},{32,0},{1,33},{33,1},{2,34},{34,2},{3,35},{35,3},{4,36},{36... | collective-permute-start | bytes 1179656 | tf_op jit(solution)/shard_map/ppermute | solution.py:133
  54.3 75.6 %copy-start.1 = (bf16[1,1,128,128,128]{4,3,2,1,0:T(8,128)(2,1)S(1)}, bf16[1,1,128,128,128]{4,3,2,1,0:T(8,128)(2,1)}, u32[]{:S(2)}) copy-start(bf16[1,1,128,128,128]{4,3,2,1,0:T(8,128)(2,1)} %param.10) | copy-start | bytes 12582916
  116.2 10.0 %collective-permute-start.2 = (bf16[13,128,128]{2,1,0:T(8,128)(2,1)S(1)}, bf16[13,128,128]{2,1,0:T(8,128)(2,1)S(1)}, u32[]{:S(2)}, u32[]{:S(2)}) collective-permute-start(bf16[13,128,128]{2,1,0:T(8,128)(2,1)S(1)} %pad_maximum_fusion.a_ref), channel_id=1, source_target_pairs={{0,32},{32,0},{1,33},{33,1},{2,34},{34,2},{3,35},{35,3},{4,36},{36... | collective-permute-start | bytes 1277960 | tf_op jit(solution)/shard_map/ppermute | solution.py:152
  119.6 8.6 %collective-permute-start.3 = (bf16[13,128,128]{2,1,0:T(8,128)(2,1)S(1)}, bf16[13,128,128]{2,1,0:T(8,128)(2,1)S(1)}, u32[]{:S(2)}, u32[]{:S(2)}) collective-permute-start(bf16[13,128,128]{2,1,0:T(8,128)(2,1)S(1)} %pad_maximum_fusion.a_ref), channel_id=1, source_target_pairs={{0,16},{16,0},{1,17},{17,1},{2,18},{18,2},{3,19},{19,3},{4,20},{20... | collective-permute-start | bytes 1277960 | tf_op jit(solution)/shard_map/ppermute | solution.py:153
  126.2 3.7 %collective-permute-start.4 = (bf16[13,128,128]{2,1,0:T(8,128)(2,1)S(1)}, bf16[13,128,128]{2,1,0:T(8,128)(2,1)S(1)}, u32[]{:S(2)}, u32[]{:S(2)}) collective-permute-start(bf16[13,128,128]{2,1,0:T(8,128)(2,1)S(1)} %collective-permute-done.2.b_ref), channel_id=1, source_target_pairs={{0,16},{16,0},{1,17},{17,1},{2,18},{18,2},{3,19},{19,3},{4,20},{20... | collective-permute-start | bytes 1277960 | tf_op jit(solution)/shard_map/ppermute | solution.py:154
